TPU v7x, 512 devices: a whole 4x8x8 slice. The times are simulated.
512 devices in a mesh: layer: 8 (over z), row: 8 (over x, core), col: 8 (over y).
Axes of the slice: x: 4, y: 8, z: 8, core: 2. Of those that a mesh axis runs over, the one named last changes fastest.
Arguments:
- c_states: float32 [8, 64, 64, 1024], P('layer', None, 'row', 'col'), may hold values from -6 to 6
- c_adjoints: float32 [8, 64, 64, 1024], P('layer', None, 'row', 'col'), may hold values from -6 to 6
- weights: bfloat16 [32, 64, 576], P('layer'), may hold values from -0.25 to 0.25
Outputs:
- new_states: float32 [8, 64, 64, 1024], P('layer', None, 'row', 'col')
- new_adjoints: float32 [8, 64, 64, 1024], P('layer', None, 'row', 'col')
- weight_grads: float32 [32, 64, 576], P('layer')
All inputs are finite; a program needn't handle non-finite values.
Results may differ from a plain program's by a relative error of at most 0.006.
Values may be sent and summed in bfloat16 or wider, within the bound.
A program may use at most 64 MiB of HBM per device.

v0:
```python
import jax
import jax.numpy as jnp
from jax import lax
from jax.sharding import PartitionSpec as P

step_size = 0.2


def with_halo(cells, sides, width):
    for axis, dim in sides:
        count = lax.axis_size(axis)
        ends = count - 1
        head = lax.slice_in_dim(cells, 0, width, axis=dim)
        tail = lax.slice_in_dim(cells, cells.shape[dim] - width, cells.shape[dim], axis=dim)
        cells = jnp.concatenate(
            [
                lax.ppermute(tail, axis, [(i, (i + 1) % count) for i in range(ends)]),
                cells,
                lax.ppermute(head, axis, [((i + 1) % count, i) for i in range(ends)]),
            ],
            axis=dim,
        )
    return cells


def from_behind(array, axis, by):
    devices = lax.axis_size(axis)
    pairs = [(i, i + by) for i in range(devices) if 0 <= i + by < devices]
    return lax.ppermute(array, axis, pairs)


def tile_patches(padded, tile_rows, tile_cols):
    shifted = [
        padded[:, row_off : row_off + tile_rows, col_off : col_off + tile_cols].reshape(
            padded.shape[0], tile_rows * tile_cols
        )
        for row_off in range(3)
        for col_off in range(3)
    ]
    return jnp.concatenate(shifted, 0)


def exact_dot(left_mat, right_mat):
    return jnp.dot(
        left_mat, right_mat, precision=lax.Precision.HIGHEST, preferred_element_type=jnp.float32
    )


def flipped(weight_mat):
    channels = weight_mat.shape[0]
    return jnp.transpose(weight_mat.reshape(channels, 9, channels)[:, ::-1, :], (2, 1, 0)).reshape(
        channels, 9 * channels
    )


def local(c_states, c_adjoints, weights):
    group_index = lax.axis_index("layer")
    group_count = lax.axis_size("layer")
    channels, tile_rows, tile_cols = c_states.shape[1:]
    pixels = tile_rows * tile_cols
    depth = weights.shape[0]
    initial_flat = c_states[0].reshape(channels, pixels)
    guess_flat = c_adjoints[0].reshape(channels, pixels)

    def advance(state, weight_mat):
        active = state.astype(jnp.bfloat16).reshape(channels, tile_rows, tile_cols)
        padded = with_halo(active, (("row", 1), ("col", 2)), 1)
        preact = jnp.dot(
            weight_mat,
            tile_patches(padded, tile_rows, tile_cols),
            preferred_element_type=jnp.float32,
        )
        return (state + step_size * jnp.tanh(preact), padded, preact)

    state = initial_flat
    for layer_pos in range(depth):
        state, _, _ = advance(state, weights[layer_pos])
    group_end = state
    summed = jnp.sum(weights[0].astype(jnp.float32).reshape(channels, 9, channels), axis=1)
    coarse_map = jnp.eye(channels, dtype=jnp.float32) + step_size * summed
    is_first = group_index == 0
    is_last = group_index == group_count - 1
    zero_map = jnp.zeros_like(coarse_map)
    blank = jnp.zeros((channels, pixels), jnp.float32)
    fwd_map = jnp.where(is_first, zero_map, coarse_map)
    fwd_offset = jnp.where(is_first, group_end, group_end - exact_dot(coarse_map, initial_flat))

    def state_turn(turn_number, carried):
        return from_behind(exact_dot(fwd_map, carried) + fwd_offset, "layer", 1)

    arrived = lax.fori_loop(0, group_count - 1, state_turn, blank)
    corrected = jnp.where(is_first, initial_flat, arrived)
    state = corrected
    trail = []
    for layer_pos in range(depth):
        state, padded, preact = advance(state, weights[layer_pos])
        trail.append((padded, preact))
    adjoint = guess_flat
    grad_list = [None] * depth
    for layer_pos in reversed(range(depth)):
        padded, preact = trail[layer_pos]
        slope = jnp.tanh(preact)
        source = (adjoint * step_size * (1.0 - slope * slope)).astype(jnp.bfloat16)
        source_pad = with_halo(
            source.reshape(channels, tile_rows, tile_cols), (("row", 1), ("col", 2)), 1
        )
        grad_list[layer_pos] = lax.dot_general(
            source,
            tile_patches(padded, tile_rows, tile_cols),
            (((1,), (1,)), ((), ())),
            preferred_element_type=jnp.float32,
        )
        back = jnp.dot(
            flipped(weights[layer_pos]),
            tile_patches(source_pad, tile_rows, tile_cols),
            preferred_element_type=jnp.float32,
        )
        adjoint = adjoint + back
    weight_grads = lax.psum(jnp.stack(grad_list, 0), ("row", "col"))
    transposed = coarse_map.T
    back_map = jnp.where(is_last, zero_map, transposed)
    back_offset = jnp.where(is_last, adjoint, adjoint - exact_dot(transposed, guess_flat))

    def adjoint_turn(turn_number, carried):
        return from_behind(exact_dot(back_map, carried) + back_offset, "layer", -1)

    returned = lax.fori_loop(0, group_count - 1, adjoint_turn, blank)
    new_adjoint = jnp.where(is_last, guess_flat, returned)
    out_shape = (1, channels, tile_rows, tile_cols)
    return (corrected.reshape(out_shape), new_adjoint.reshape(out_shape), weight_grads)


def solution(mesh):
    placed = (
        P("layer", None, "row", "col"),
        P("layer", None, "row", "col"),
        P("layer", None, None),
    )
    return jax.shard_map(
        local,
        mesh=mesh,
        in_specs=placed,
        out_specs=(
            P("layer", None, "row", "col"),
            P("layer", None, "row", "col"),
            P("layer", None, None),
        ),
        check_vma=False,
    )
```

profile of v0, /device:TPU:1, one launch (start us, length us, event | category | flops | bytes accessed | tf_op | source)
XLA Modules:
  0.0 560.1 jit_solution(8448254401400745606)
XLA Ops:
  12.8 5.6 collective-permute-start.3
  22.8 4.6 collective-permute-done.4
  64.7 5.2 collective-permute-start.12
  74.9 4.8 collective-permute-done.13
  105.2 64.2 %while.20 = (s32[]{:T(128)}, f32[64,1024]{1,0:T(8,128)S(1)}, f32[64,64]{1,0:T(8,128)S(1)}, f32[64,1024]{1,0:T(8,128)S(1)}, s32[]{:T(128)}) while((s32[]{:T(128)}, f32[64,1024]{1,0:T(8,128)S(1)}, f32[64,64]{1,0:T(8,128)S(1)}, f32[64,1024]{1,0:T(8,128)S(1)}, s32[]{:T(128)}) %tuple.143), condition=%wide.region_2.3_spmd, body=%wide.region_1.2_spmd.sunk | while | flops 50397184 | bytes 1851493 | solution.py:91
  109.6 5.8 %collective-permute-done = f32[64,1024]{1,0:T(8,128)S(1)} collective-permute-done((f32[64,1024]{1,0:T(8,128)S(1)}, f32[64,1024]{1,0:T(8,128)S(1)}, u32[]{:S(2)}, u32[]{:S(2)}) %collective-permute-start) | collective-permute-done | bytes 262176 | tf_op jit(solution)/shard_map/while/body/eval_jaxpr/ppermute | solution.py:29
  119.8 5.5 collective-permute-done
  129.8 4.5 collective-permute-done
  134.7 5.4 collective-permute-start
  152.0 5.1 collective-permute-start
  160.8 5.3 collective-permute-start
  169.5 6.1 %collective-permute-start.18 = (bf16[64,1,128]{2,1,0:T(2,128)(2,1)S(1)}, bf16[64,1,128]{2,1,0:T(2,128)(2,1)S(1)}, u32[]{:S(2)}, u32[]{:S(2)}) collective-permute-start(bf16[64,1,128]{2,1,0:T(2,128)(2,1)S(1)} %get-tuple-element.215), channel_id=1, source_target_pairs={{0,8},{8,16},{16,24},{24,32},{32,40},{40,48},{48,56},{1,9},{9,17},... | collective-permute-start | bytes 49160 | tf_op jit(solution)/shard_map/ppermute | solution.py:17
  211.0 4.6 collective-permute-done.25
  288.2 6.2 %collective-permute-done.37 = bf16[64,10,1]{2,1,0:T(8,128)(2,1)S(1)} collective-permute-done((bf16[64,10,1]{2,1,0:T(8,128)(2,1)}, bf16[64,10,1]{2,1,0:T(8,128)(2,1)S(1)}, u32[]{:S(2)}, u32[]{:S(2)}) %collective-permute-start.37) | collective-permute-done | bytes 1312 | tf_op jit(solution)/shard_map/ppermute | solution.py:19
  362.3 4.5 collective-permute-done.49
  369.2 71.1 %while.21 = (s32[]{:T(128)}, f32[64,1024]{1,0:T(8,128)S(1)}, f32[64,64]{1,0:T(8,128)S(1)}, f32[64,1024]{1,0:T(8,128)S(1)}, s32[]{:T(128)}) while((s32[]{:T(128)}, f32[64,1024]{1,0:T(8,128)S(1)}, f32[64,64]{1,0:T(8,128)S(1)}, f32[64,1024]{1,0:T(8,128)S(1)}, s32[]{:T(128)}) %tuple.146), condition=%wide.region_4.5_spmd, body=%wide.region_3.4_spmd.sunk | while | flops 50397184 | bytes 1851493 | solution.py:127
  370.9 10.6 %collective-permute-done.1 = f32[64,1024]{1,0:T(8,128)S(1)} collective-permute-done((f32[64,1024]{1,0:T(8,128)S(1)}, f32[64,1024]{1,0:T(8,128)S(1)}, u32[]{:S(2)}, u32[]{:S(2)}) %collective-permute-start.1) | collective-permute-done | bytes 262176 | tf_op jit(solution)/shard_map/while/body/eval_jaxpr/ppermute | solution.py:29
  383.2 10.7 %collective-permute-done.1 = f32[64,1024]{1,0:T(8,128)S(1)} collective-permute-done((f32[64,1024]{1,0:T(8,128)S(1)}, f32[64,1024]{1,0:T(8,128)S(1)}, u32[]{:S(2)}, u32[]{:S(2)}) %collective-permute-start.1) | collective-permute-done | bytes 262176 | tf_op jit(solution)/shard_map/while/body/eval_jaxpr/ppermute | solution.py:29
  395.6 10.1 %collective-permute-done.1 = f32[64,1024]{1,0:T(8,128)S(1)} collective-permute-done((f32[64,1024]{1,0:T(8,128)S(1)}, f32[64,1024]{1,0:T(8,128)S(1)}, u32[]{:S(2)}, u32[]{:S(2)}) %collective-permute-start.1) | collective-permute-done | bytes 262176 | tf_op jit(solution)/shard_map/while/body/eval_jaxpr/ppermute | solution.py:29
  407.3 9.0 %collective-permute-done.1 = f32[64,1024]{1,0:T(8,128)S(1)} collective-permute-done((f32[64,1024]{1,0:T(8,128)S(1)}, f32[64,1024]{1,0:T(8,128)S(1)}, u32[]{:S(2)}, u32[]{:S(2)}) %collective-permute-start.1) | collective-permute-done | bytes 262176 | tf_op jit(solution)/shard_map/while/body/eval_jaxpr/ppermute | solution.py:29
  418.0 6.4 %collective-permute-done.1 = f32[64,1024]{1,0:T(8,128)S(1)} collective-permute-done((f32[64,1024]{1,0:T(8,128)S(1)}, f32[64,1024]{1,0:T(8,128)S(1)}, u32[]{:S(2)}, u32[]{:S(2)}) %collective-permute-start.1) | collective-permute-done | bytes 262176 | tf_op jit(solution)/shard_map/while/body/eval_jaxpr/ppermute | solution.py:29
  426.1 5.8 %collective-permute-done.1 = f32[64,1024]{1,0:T(8,128)S(1)} collective-permute-done((f32[64,1024]{1,0:T(8,128)S(1)}, f32[64,1024]{1,0:T(8,128)S(1)}, u32[]{:S(2)}, u32[]{:S(2)}) %collective-permute-start.1) | collective-permute-done | bytes 262176 | tf_op jit(solution)/shard_map/while/body/eval_jaxpr/ppermute | solution.py:29
  433.5 6.8 %collective-permute-done.1 = f32[64,1024]{1,0:T(8,128)S(1)} collective-permute-done((f32[64,1024]{1,0:T(8,128)S(1)}, f32[64,1024]{1,0:T(8,128)S(1)}, u32[]{:S(2)}, u32[]{:S(2)}) %collective-permute-start.1) | collective-permute-done | bytes 262176 | tf_op jit(solution)/shard_map/while/body/eval_jaxpr/ppermute | solution.py:29
  441.1 110.2 %all-reduce.2.cloned.1.call-done = f32[4,64,576]{2,1,0:T(8,128)} async-done(((f32[4,64,576]{2,1,0:T(8,128)}), f32[4,64,576]{2,1,0:T(8,128)}) %all-reduce.2.cloned.1.call-update) | async-done | bytes 589840 | tf_op jit(solution)/shard_map/psum | solution.py:119
  (400 shorter events, 300.9 us)
Async XLA Ops:
  7.2 544.2 %all-reduce.2.cloned.1.call-start = ((), (), s32[]{:S(2)}) async-start(), calls=%async_computation | async-start | bytes 1310720 | tf_op jit(solution)/shard_map/psum | solution.py:119
  8.2 10.1 %collective-permute-start.2 = (bf16[64,1,128]{2,1,0:T(2,128)(2,1)S(1)}, bf16[64,1,128]{2,1,0:T(2,128)(2,1)S(1)}, u32[]{:S(2)}, u32[]{:S(2)}) collective-permute-start(bf16[64,1,128]{2,1,0:T(2,128)(2,1)S(1)} %get-tuple-element.223), channel_id=1, source_target_pairs={{0,8},{8,16},{16,24},{24,32},{32,40},{40,48},{48,56},{1,9},{9,17},... | collective-permute-start | bytes 49160 | tf_op jit(solution)/shard_map/ppermute | solution.py:17
  21.5 10.1 %collective-permute-start.5 = (bf16[64,10,1]{2,1,0:T(8,128)(2,1)S(1)}, bf16[64,10,1]{2,1,0:T(8,128)(2,1)S(1)}, u32[]{:S(2)}, u32[]{:S(2)}) collective-permute-start(bf16[64,10,1]{2,1,0:T(8,128)(2,1)S(1)} %get-tuple-element.175), channel_id=1, source_target_pairs={{1,0},{2,1},{3,2},{4,3},{5,4},{6,5},{7,6},{9,8},{10,9},{11,10},{12... | collective-permute-start | bytes 3848 | tf_op jit(solution)/shard_map/ppermute | solution.py:19
  64.7 9.7 %collective-permute-start.12 = (bf16[64,10,1]{2,1,0:T(8,128)(2,1)S(1)}, bf16[64,10,1]{2,1,0:T(8,128)(2,1)S(1)}, u32[]{:S(2)}, u32[]{:S(2)}) collective-permute-start(bf16[64,10,1]{2,1,0:T(8,128)(2,1)S(1)} %get-tuple-element.172), channel_id=1, source_target_pairs={{0,1},{1,2},{2,3},{3,4},{4,5},{5,6},{6,7},{8,9},{9,10},{10,11},{11... | collective-permute-start | bytes 3848 | tf_op jit(solution)/shard_map/ppermute | solution.py:17
  70.8 8.9 %collective-permute-start.13 = (bf16[64,10,1]{2,1,0:T(8,128)(2,1)S(1)}, bf16[64,10,1]{2,1,0:T(8,128)(2,1)S(1)}, u32[]{:S(2)}, u32[]{:S(2)}) collective-permute-start(bf16[64,10,1]{2,1,0:T(8,128)(2,1)S(1)} %get-tuple-element.171), channel_id=1, source_target_pairs={{1,0},{2,1},{3,2},{4,3},{5,4},{6,5},{7,6},{9,8},{10,9},{11,10},{12... | collective-permute-start | bytes 3848 | tf_op jit(solution)/shard_map/ppermute | solution.py:19
  105.6 9.8 %collective-permute-start = (f32[64,1024]{1,0:T(8,128)S(1)}, f32[64,1024]{1,0:T(8,128)S(1)}, u32[]{:S(2)}, u32[]{:S(2)}) collective-permute-start(f32[64,1024]{1,0:T(8,128)S(1)} %convolution_add_fusion.4), channel_id=1, source_target_pairs={{0,64},{64,128},{128,192},{192,256},{256,320},{320,384},{384,448},... | collective-permute-start | bytes 786440 | tf_op jit(solution)/shard_map/while/body/eval_jaxpr/ppermute | solution.py:29
  115.8 9.5 %collective-permute-start = (f32[64,1024]{1,0:T(8,128)S(1)}, f32[64,1024]{1,0:T(8,128)S(1)}, u32[]{:S(2)}, u32[]{:S(2)}) collective-permute-start(f32[64,1024]{1,0:T(8,128)S(1)} %convolution_add_fusion.4), channel_id=1, source_target_pairs={{0,64},{64,128},{128,192},{192,256},{256,320},{320,384},{384,448},... | collective-permute-start | bytes 786440 | tf_op jit(solution)/shard_map/while/body/eval_jaxpr/ppermute | solution.py:29
  125.7 8.7 %collective-permute-start = (f32[64,1024]{1,0:T(8,128)S(1)}, f32[64,1024]{1,0:T(8,128)S(1)}, u32[]{:S(2)}, u32[]{:S(2)}) collective-permute-start(f32[64,1024]{1,0:T(8,128)S(1)} %convolution_add_fusion.4), channel_id=1, source_target_pairs={{0,64},{64,128},{128,192},{192,256},{256,320},{320,384},{384,448},... | collective-permute-start | bytes 786440 | tf_op jit(solution)/shard_map/while/body/eval_jaxpr/ppermute | solution.py:29
  134.7 9.2 %collective-permute-start = (f32[64,1024]{1,0:T(8,128)S(1)}, f32[64,1024]{1,0:T(8,128)S(1)}, u32[]{:S(2)}, u32[]{:S(2)}) collective-permute-start(f32[64,1024]{1,0:T(8,128)S(1)} %convolution_add_fusion.4), channel_id=1, source_target_pairs={{0,64},{64,128},{128,192},{192,256},{256,320},{320,384},{384,448},... | collective-permute-start | bytes 786440 | tf_op jit(solution)/shard_map/while/body/eval_jaxpr/ppermute | solution.py:29
  169.5 9.0 %collective-permute-start.18 = (bf16[64,1,128]{2,1,0:T(2,128)(2,1)S(1)}, bf16[64,1,128]{2,1,0:T(2,128)(2,1)S(1)}, u32[]{:S(2)}, u32[]{:S(2)}) collective-permute-start(bf16[64,1,128]{2,1,0:T(2,128)(2,1)S(1)} %get-tuple-element.215), channel_id=1, source_target_pairs={{0,8},{8,16},{16,24},{24,32},{32,40},{40,48},{48,56},{1,9},{9,17},... | collective-permute-start | bytes 49160 | tf_op jit(solution)/shard_map/ppermute | solution.py:17
  183.5 9.3 %collective-permute-start.21 = (bf16[64,10,1]{2,1,0:T(8,128)(2,1)S(1)}, bf16[64,10,1]{2,1,0:T(8,128)(2,1)S(1)}, u32[]{:S(2)}, u32[]{:S(2)}) collective-permute-start(bf16[64,10,1]{2,1,0:T(8,128)(2,1)S(1)} %get-tuple-element.167), channel_id=1, source_target_pairs={{1,0},{2,1},{3,2},{4,3},{5,4},{6,5},{7,6},{9,8},{10,9},{11,10},{12... | collective-permute-start | bytes 3848 | tf_op jit(solution)/shard_map/ppermute | solution.py:19
  206.1 9.6 %collective-permute-start.25 = (bf16[64,10,1]{2,1,0:T(8,128)(2,1)S(1)}, bf16[64,10,1]{2,1,0:T(8,128)(2,1)S(1)}, u32[]{:S(2)}, u32[]{:S(2)}) collective-permute-start(bf16[64,10,1]{2,1,0:T(8,128)(2,1)S(1)} %get-tuple-element.165), channel_id=1, source_target_pairs={{1,0},{2,1},{3,2},{4,3},{5,4},{6,5},{7,6},{9,8},{10,9},{11,10},{12... | collective-permute-start | bytes 3848 | tf_op jit(solution)/shard_map/ppermute | solution.py:19
  231.7 8.7 %collective-permute-start.29 = (bf16[64,10,1]{2,1,0:T(8,128)(2,1)}, bf16[64,10,1]{2,1,0:T(8,128)(2,1)S(1)}, u32[]{:S(2)}, u32[]{:S(2)}) collective-permute-start(bf16[64,10,1]{2,1,0:T(8,128)(2,1)} %get-tuple-element.163), channel_id=1, source_target_pairs={{1,0},{2,1},{3,2},{4,3},{5,4},{6,5},{7,6},{9,8},{10,9},{11,10},{12... | collective-permute-start | bytes 3848 | tf_op jit(solution)/shard_map/ppermute | solution.py:19
  255.7 8.7 %collective-permute-start.33 = (bf16[64,10,1]{2,1,0:T(8,128)(2,1)}, bf16[64,10,1]{2,1,0:T(8,128)(2,1)S(1)}, u32[]{:S(2)}, u32[]{:S(2)}) collective-permute-start(bf16[64,10,1]{2,1,0:T(8,128)(2,1)} %get-tuple-element.161), channel_id=1, source_target_pairs={{1,0},{2,1},{3,2},{4,3},{5,4},{6,5},{7,6},{9,8},{10,9},{11,10},{12... | collective-permute-start | bytes 3848 | tf_op jit(solution)/shard_map/ppermute | solution.py:19
  277.7 8.7 %collective-permute-start.36 = (bf16[64,10,1]{2,1,0:T(8,128)(2,1)}, bf16[64,10,1]{2,1,0:T(8,128)(2,1)}, u32[]{:S(2)}, u32[]{:S(2)}) collective-permute-start(bf16[64,10,1]{2,1,0:T(8,128)(2,1)} %get-tuple-element.160), channel_id=1, source_target_pairs={{0,1},{1,2},{2,3},{3,4},{4,5},{5,6},{6,7},{8,9},{9,10},{10,11},{11... | collective-permute-start | bytes 3848 | tf_op jit(solution)/shard_map/ppermute | solution.py:17
  285.2 9.3 %collective-permute-start.37 = (bf16[64,10,1]{2,1,0:T(8,128)(2,1)}, bf16[64,10,1]{2,1,0:T(8,128)(2,1)S(1)}, u32[]{:S(2)}, u32[]{:S(2)}) collective-permute-start(bf16[64,10,1]{2,1,0:T(8,128)(2,1)} %get-tuple-element.159), channel_id=1, source_target_pairs={{1,0},{2,1},{3,2},{4,3},{5,4},{6,5},{7,6},{9,8},{10,9},{11,10},{12... | collective-permute-start | bytes 3848 | tf_op jit(solution)/shard_map/ppermute | solution.py:19
  298.8 9.9 %collective-permute-start.38 = (bf16[64,1,128]{2,1,0:T(2,128)(2,1)}, bf16[64,1,128]{2,1,0:T(2,128)(2,1)S(1)}, u32[]{:S(2)}, u32[]{:S(2)}) collective-permute-start(bf16[64,1,128]{2,1,0:T(2,128)(2,1)} %get-tuple-element.205), channel_id=1, source_target_pairs={{0,8},{8,16},{16,24},{24,32},{32,40},{40,48},{48,56},{1,9},{9,17},... | collective-permute-start | bytes 49160 | tf_op jit(solution)/shard_map/ppermute | solution.py:17
  312.0 10.1 %collective-permute-start.41 = (bf16[64,10,1]{2,1,0:T(8,128)(2,1)S(1)}, bf16[64,10,1]{2,1,0:T(8,128)(2,1)S(1)}, u32[]{:S(2)}, u32[]{:S(2)}) collective-permute-start(bf16[64,10,1]{2,1,0:T(8,128)(2,1)S(1)} %get-tuple-element.157), channel_id=1, source_target_pairs={{1,0},{2,1},{3,2},{4,3},{5,4},{6,5},{7,6},{9,8},{10,9},{11,10},{12... | collective-permute-start | bytes 3848 | tf_op jit(solution)/shard_map/ppermute | solution.py:19
  335.4 9.0 %collective-permute-start.45 = (bf16[64,10,1]{2,1,0:T(8,128)(2,1)S(1)}, bf16[64,10,1]{2,1,0:T(8,128)(2,1)S(1)}, u32[]{:S(2)}, u32[]{:S(2)}) collective-permute-start(bf16[64,10,1]{2,1,0:T(8,128)(2,1)S(1)} %get-tuple-element.155), channel_id=1, source_target_pairs={{1,0},{2,1},{3,2},{4,3},{5,4},{6,5},{7,6},{9,8},{10,9},{11,10},{12... | collective-permute-start | bytes 3848 | tf_op jit(solution)/shard_map/ppermute | solution.py:19
  357.8 9.0 %collective-permute-start.49 = (bf16[64,10,1]{2,1,0:T(8,128)(2,1)S(1)}, bf16[64,10,1]{2,1,0:T(8,128)(2,1)S(1)}, u32[]{:S(2)}, u32[]{:S(2)}) collective-permute-start(bf16[64,10,1]{2,1,0:T(8,128)(2,1)S(1)} %get-tuple-element.153), channel_id=1, source_target_pairs={{1,0},{2,1},{3,2},{4,3},{5,4},{6,5},{7,6},{9,8},{10,9},{11,10},{12... | collective-permute-start | bytes 3848 | tf_op jit(solution)/shard_map/ppermute | solution.py:19
  369.6 11.9 %collective-permute-start.1 = (f32[64,1024]{1,0:T(8,128)S(1)}, f32[64,1024]{1,0:T(8,128)S(1)}, u32[]{:S(2)}, u32[]{:S(2)}) collective-permute-start(f32[64,1024]{1,0:T(8,128)S(1)} %convolution_add_fusion.5), channel_id=1, source_target_pairs={{64,0},{128,64},{192,128},{256,192},{320,256},{384,320},{448,384},... | collective-permute-start | bytes 786440 | tf_op jit(solution)/shard_map/while/body/eval_jaxpr/ppermute | solution.py:29
  381.9 12.0 %collective-permute-start.1 = (f32[64,1024]{1,0:T(8,128)S(1)}, f32[64,1024]{1,0:T(8,128)S(1)}, u32[]{:S(2)}, u32[]{:S(2)}) collective-permute-start(f32[64,1024]{1,0:T(8,128)S(1)} %convolution_add_fusion.5), channel_id=1, source_target_pairs={{64,0},{128,64},{192,128},{256,192},{320,256},{384,320},{448,384},... | collective-permute-start | bytes 786440 | tf_op jit(solution)/shard_map/while/body/eval_jaxpr/ppermute | solution.py:29
  394.3 11.4 %collective-permute-start.1 = (f32[64,1024]{1,0:T(8,128)S(1)}, f32[64,1024]{1,0:T(8,128)S(1)}, u32[]{:S(2)}, u32[]{:S(2)}) collective-permute-start(f32[64,1024]{1,0:T(8,128)S(1)} %convolution_add_fusion.5), channel_id=1, source_target_pairs={{64,0},{128,64},{192,128},{256,192},{320,256},{384,320},{448,384},... | collective-permute-start | bytes 786440 | tf_op jit(solution)/shard_map/while/body/eval_jaxpr/ppermute | solution.py:29
  406.0 10.3 %collective-permute-start.1 = (f32[64,1024]{1,0:T(8,128)S(1)}, f32[64,1024]{1,0:T(8,128)S(1)}, u32[]{:S(2)}, u32[]{:S(2)}) collective-permute-start(f32[64,1024]{1,0:T(8,128)S(1)} %convolution_add_fusion.5), channel_id=1, source_target_pairs={{64,0},{128,64},{192,128},{256,192},{320,256},{384,320},{448,384},... | collective-permute-start | bytes 786440 | tf_op jit(solution)/shard_map/while/body/eval_jaxpr/ppermute | solution.py:29
  (66 other events, 419.7 us)
Sparse Core Ops, SparseCore 0:
  357.9 193.3 all-reduce.1
where the time goes:
time: 563 us; the launch traced here: 560 us
  waiting for transfers between devices  312 us (55%)
  starting transfers between devices  164 us (29%)
  local copies, waits for them, and re-layouts  28.5 us (5%)
  other arithmetic  24.9 us (4%)
  between operations  16.1 us (3%)
  matrix products  13.7 us (2%)
    psum x1, waiting for transfers between devices, local(): weight_grads = lax.psum(jnp.stack(grad_list, 0), ('row', 'col'))  110 us
    ppermute x14, waiting for transfers between devices, from_behind(): return lax.ppermute(array, axis, pairs)  88.8 us
    ppermute x24, waiting for transfers between devices, with_halo(): lax.ppermute(head, axis, [((i + 1) % count, i) for i in range(ends)])  78.5 us
    ppermute x24, starting transfers between devices, with_halo(): lax.ppermute(tail, axis, [(i, (i + 1) % count) for i in range(ends)])  77.9 us
    ppermute x24, starting transfers between devices, with_halo(): lax.ppermute(head, axis, [((i + 1) % count, i) for i in range(ends)])  45.4 us
    ppermute x14, starting transfers between devices, from_behind(): return lax.ppermute(array, axis, pairs)  41.1 us
    ppermute x24, waiting for transfers between devices, with_halo(): lax.ppermute(tail, axis, [(i, (i + 1) % count) for i in range(ends)])  34.7 us
    concatenate x36, other arithmetic, with_halo(): jnp.concatenate([lax.ppermute(tail, axis, [(i, (i + 1) % count) for i in...  21.9 us
  transfers between devices with their start and end apart: 63, of which 49 were waited for; matrix products, arithmetic and copies ran while one was open for 5% of the time, Pallas kernels for 0%

commit v1 on v0

--- a/solution.py
+++ b/solution.py
@@ -116,7 +116,7 @@
             preferred_element_type=jnp.float32,
         )
         adjoint = adjoint + back
-    weight_grads = lax.psum(jnp.stack(grad_list, 0), ("row", "col"))
+    weight_grads = lax.psum(lax.psum(jnp.stack(grad_list, 0), "col"), "row")
     transposed = coarse_map.T
     back_map = jnp.where(is_last, zero_map, transposed)
     back_offset = jnp.where(is_last, adjoint, adjoint - exact_dot(transposed, guess_flat))

time: 563 us -> 525 us (0.933)
  waiting for transfers between devices: 312 us -> 273 us
    psum x1 -> x2, waiting for transfers between devices: 110 us -> 73.7 us  [local(): weight_grads = lax.psum(lax.psum(jnp.stack(grad_list, 0), 'col'), 'row')]
  transfers between devices with their start and end apart: 63 -> 64, of which waited for: 49 -> 50; matrix products, arithmetic and copies ran while one was open for 5% -> 6% of each run, Pallas kernels for 0% -> 0%
where the time goes in v1:
time: 525 us; the launch traced here: 520 us
  waiting for transfers between devices  273 us (52%)
  starting transfers between devices  164 us (31%)
  local copies, waits for them, and re-layouts  28.5 us (5%)
  other arithmetic  23.8 us (5%)
  between operations  16.2 us (3%)
  matrix products  13.6 us (3%)
    ppermute x14, waiting for transfers between devices, from_behind(): return lax.ppermute(array, axis, pairs)  85.1 us
    ppermute x24, waiting for transfers between devices, with_halo(): lax.ppermute(head, axis, [((i + 1) % count, i) for i in range(ends)])  79.1 us
    ppermute x24, starting transfers between devices, with_halo(): lax.ppermute(tail, axis, [(i, (i + 1) % count) for i in range(ends)])  77.1 us
    psum x2, waiting for transfers between devices, local(): weight_grads = lax.psum(lax.psum(jnp.stack(grad_list, 0), 'col'), 'row')  73.7 us
    ppermute x24, starting transfers between devices, with_halo(): lax.ppermute(head, axis, [((i + 1) % count, i) for i in range(ends)])  45.3 us
    ppermute x14, starting transfers between devices, from_behind(): return lax.ppermute(array, axis, pairs)  41.3 us
    ppermute x24, waiting for transfers between devices, with_halo(): lax.ppermute(tail, axis, [(i, (i + 1) % count) for i in range(ends)])  35.5 us
    concatenate x36, other arithmetic, with_halo(): jnp.concatenate([lax.ppermute(tail, axis, [(i, (i + 1) % count) for i in...  20.8 us
  transfers between devices with their start and end apart: 64, of which 50 were waited for; matrix products, arithmetic and copies ran while one was open for 6% of the time, Pallas kernels for 0%

profile of v1, /device:TPU:1, one launch (start us, length us, event | category | flops | bytes accessed | tf_op | source)
XLA Modules:
  0.0 519.5 jit_solution(5315430859390355206)
XLA Ops:
  12.8 5.6 %collective-permute-start.3 = (bf16[64,1,128]{2,1,0:T(2,128)(2,1)S(1)}, bf16[64,1,128]{2,1,0:T(2,128)(2,1)S(1)}, u32[]{:S(2)}, u32[]{:S(2)}) collective-permute-start(bf16[64,1,128]{2,1,0:T(2,128)(2,1)S(1)} %get-tuple-element.224), channel_id=1, source_target_pairs={{8,0},{16,8},{24,16},{32,24},{40,32},{48,40},{56,48},{9,1},{17,9},... | collective-permute-start | bytes 49160 | tf_op jit(solution)/shard_map/ppermute | solution.py:19
  22.8 4.6 collective-permute-done.4
  64.7 5.2 %collective-permute-start.12 = (bf16[64,10,1]{2,1,0:T(8,128)(2,1)S(1)}, bf16[64,10,1]{2,1,0:T(8,128)(2,1)S(1)}, u32[]{:S(2)}, u32[]{:S(2)}) collective-permute-start(bf16[64,10,1]{2,1,0:T(8,128)(2,1)S(1)} %get-tuple-element.172), channel_id=1, source_target_pairs={{0,1},{1,2},{2,3},{3,4},{4,5},{5,6},{6,7},{8,9},{9,10},{10,11},{11... | collective-permute-start | bytes 3848 | tf_op jit(solution)/shard_map/ppermute | solution.py:17
  74.9 4.8 collective-permute-done.13
  105.2 64.1 %while.20 = (s32[]{:T(128)}, f32[64,1024]{1,0:T(8,128)S(1)}, f32[64,64]{1,0:T(8,128)S(1)}, f32[64,1024]{1,0:T(8,128)S(1)}, s32[]{:T(128)}) while((s32[]{:T(128)}, f32[64,1024]{1,0:T(8,128)S(1)}, f32[64,64]{1,0:T(8,128)S(1)}, f32[64,1024]{1,0:T(8,128)S(1)}, s32[]{:T(128)}) %tuple.143), condition=%wide.region_2.3_spmd, body=%wide.region_1.2_spmd.sunk | while | flops 50397184 | bytes 1851493 | solution.py:91
  109.6 5.8 %collective-permute-done = f32[64,1024]{1,0:T(8,128)S(1)} collective-permute-done((f32[64,1024]{1,0:T(8,128)S(1)}, f32[64,1024]{1,0:T(8,128)S(1)}, u32[]{:S(2)}, u32[]{:S(2)}) %collective-permute-start) | collective-permute-done | bytes 262176 | tf_op jit(solution)/shard_map/while/body/eval_jaxpr/ppermute | solution.py:29
  119.8 5.4 %collective-permute-done = f32[64,1024]{1,0:T(8,128)S(1)} collective-permute-done((f32[64,1024]{1,0:T(8,128)S(1)}, f32[64,1024]{1,0:T(8,128)S(1)}, u32[]{:S(2)}, u32[]{:S(2)}) %collective-permute-start) | collective-permute-done | bytes 262176 | tf_op jit(solution)/shard_map/while/body/eval_jaxpr/ppermute | solution.py:29
  134.6 5.4 %collective-permute-start = (f32[64,1024]{1,0:T(8,128)S(1)}, f32[64,1024]{1,0:T(8,128)S(1)}, u32[]{:S(2)}, u32[]{:S(2)}) collective-permute-start(f32[64,1024]{1,0:T(8,128)S(1)} %convolution_add_fusion.4), channel_id=1, source_target_pairs={{0,64},{64,128},{128,192},{192,256},{256,320},{320,384},{384,448},... | collective-permute-start | bytes 786440 | tf_op jit(solution)/shard_map/while/body/eval_jaxpr/ppermute | solution.py:29
  151.8 5.3 %collective-permute-start = (f32[64,1024]{1,0:T(8,128)S(1)}, f32[64,1024]{1,0:T(8,128)S(1)}, u32[]{:S(2)}, u32[]{:S(2)}) collective-permute-start(f32[64,1024]{1,0:T(8,128)S(1)} %convolution_add_fusion.4), channel_id=1, source_target_pairs={{0,64},{64,128},{128,192},{192,256},{256,320},{320,384},{384,448},... | collective-permute-start | bytes 786440 | tf_op jit(solution)/shard_map/while/body/eval_jaxpr/ppermute | solution.py:29
  160.8 5.3 %collective-permute-start = (f32[64,1024]{1,0:T(8,128)S(1)}, f32[64,1024]{1,0:T(8,128)S(1)}, u32[]{:S(2)}, u32[]{:S(2)}) collective-permute-start(f32[64,1024]{1,0:T(8,128)S(1)} %convolution_add_fusion.4), channel_id=1, source_target_pairs={{0,64},{64,128},{128,192},{192,256},{256,320},{320,384},{384,448},... | collective-permute-start | bytes 786440 | tf_op jit(solution)/shard_map/while/body/eval_jaxpr/ppermute | solution.py:29
  169.5 6.1 %collective-permute-start.18 = (bf16[64,1,128]{2,1,0:T(2,128)(2,1)S(1)}, bf16[64,1,128]{2,1,0:T(2,128)(2,1)S(1)}, u32[]{:S(2)}, u32[]{:S(2)}) collective-permute-start(bf16[64,1,128]{2,1,0:T(2,128)(2,1)S(1)} %get-tuple-element.215), channel_id=1, source_target_pairs={{0,8},{8,16},{16,24},{24,32},{32,40},{40,48},{48,56},{1,9},{9,17},... | collective-permute-start | bytes 49160 | tf_op jit(solution)/shard_map/ppermute | solution.py:17
  210.9 4.8 collective-permute-done.25
  288.0 6.2 %collective-permute-done.37 = bf16[64,10,1]{2,1,0:T(8,128)(2,1)S(1)} collective-permute-done((bf16[64,10,1]{2,1,0:T(8,128)(2,1)}, bf16[64,10,1]{2,1,0:T(8,128)(2,1)S(1)}, u32[]{:S(2)}, u32[]{:S(2)}) %collective-permute-start.37) | collective-permute-done | bytes 1312 | tf_op jit(solution)/shard_map/ppermute | solution.py:19
  361.7 4.6 collective-permute-done.49
  368.6 65.9 %all-reduce.3.cloned.1.call-done = f32[4,64,576]{2,1,0:T(8,128)} async-done(((f32[4,64,576]{2,1,0:T(8,128)}), f32[4,64,576]{2,1,0:T(8,128)}) %all-reduce.3.cloned.1.call-update) | async-done | bytes 589840 | tf_op jit(solution)/shard_map/psum | solution.py:119
  434.6 67.5 %while.21 = (s32[]{:T(128)}, f32[64,1024]{1,0:T(8,128)S(1)}, f32[64,64]{1,0:T(8,128)S(1)}, f32[64,1024]{1,0:T(8,128)S(1)}, s32[]{:T(128)}) while((s32[]{:T(128)}, f32[64,1024]{1,0:T(8,128)S(1)}, f32[64,64]{1,0:T(8,128)S(1)}, f32[64,1024]{1,0:T(8,128)S(1)}, s32[]{:T(128)}) %tuple.146), condition=%wide.region_4.5_spmd, body=%wide.region_3.4_spmd.sunk | while | flops 50397184 | bytes 1851493 | solution.py:127
  436.3 5.8 %collective-permute-done.1 = f32[64,1024]{1,0:T(8,128)S(1)} collective-permute-done((f32[64,1024]{1,0:T(8,128)S(1)}, f32[64,1024]{1,0:T(8,128)S(1)}, u32[]{:S(2)}, u32[]{:S(2)}) %collective-permute-start.1) | collective-permute-done | bytes 262176 | tf_op jit(solution)/shard_map/while/body/eval_jaxpr/ppermute | solution.py:29
  443.8 6.8 %collective-permute-done.1 = f32[64,1024]{1,0:T(8,128)S(1)} collective-permute-done((f32[64,1024]{1,0:T(8,128)S(1)}, f32[64,1024]{1,0:T(8,128)S(1)}, u32[]{:S(2)}, u32[]{:S(2)}) %collective-permute-start.1) | collective-permute-done | bytes 262176 | tf_op jit(solution)/shard_map/while/body/eval_jaxpr/ppermute | solution.py:29
  452.2 8.3 %collective-permute-done.1 = f32[64,1024]{1,0:T(8,128)S(1)} collective-permute-done((f32[64,1024]{1,0:T(8,128)S(1)}, f32[64,1024]{1,0:T(8,128)S(1)}, u32[]{:S(2)}, u32[]{:S(2)}) %collective-permute-start.1) | collective-permute-done | bytes 262176 | tf_op jit(solution)/shard_map/while/body/eval_jaxpr/ppermute | solution.py:29
  462.2 8.9 %collective-permute-done.1 = f32[64,1024]{1,0:T(8,128)S(1)} collective-permute-done((f32[64,1024]{1,0:T(8,128)S(1)}, f32[64,1024]{1,0:T(8,128)S(1)}, u32[]{:S(2)}, u32[]{:S(2)}) %collective-permute-start.1) | collective-permute-done | bytes 262176 | tf_op jit(solution)/shard_map/while/body/eval_jaxpr/ppermute | solution.py:29
  472.7 8.0 %collective-permute-done.1 = f32[64,1024]{1,0:T(8,128)S(1)} collective-permute-done((f32[64,1024]{1,0:T(8,128)S(1)}, f32[64,1024]{1,0:T(8,128)S(1)}, u32[]{:S(2)}, u32[]{:S(2)}) %collective-permute-start.1) | collective-permute-done | bytes 262176 | tf_op jit(solution)/shard_map/while/body/eval_jaxpr/ppermute | solution.py:29
  482.4 8.0 %collective-permute-done.1 = f32[64,1024]{1,0:T(8,128)S(1)} collective-permute-done((f32[64,1024]{1,0:T(8,128)S(1)}, f32[64,1024]{1,0:T(8,128)S(1)}, u32[]{:S(2)}, u32[]{:S(2)}) %collective-permute-start.1) | collective-permute-done | bytes 262176 | tf_op jit(solution)/shard_map/while/body/eval_jaxpr/ppermute | solution.py:29
  492.1 10.1 %collective-permute-done.1 = f32[64,1024]{1,0:T(8,128)S(1)} collective-permute-done((f32[64,1024]{1,0:T(8,128)S(1)}, f32[64,1024]{1,0:T(8,128)S(1)}, u32[]{:S(2)}, u32[]{:S(2)}) %collective-permute-start.1) | collective-permute-done | bytes 262176 | tf_op jit(solution)/shard_map/while/body/eval_jaxpr/ppermute | solution.py:29
  503.0 7.7 %all-reduce.5.cloned.1.call-done = f32[4,64,576]{2,1,0:T(8,128)} async-done(((f32[4,64,576]{2,1,0:T(8,128)}), f32[4,64,576]{2,1,0:T(8,128)}) %all-reduce.5.cloned.1.call-update) | async-done | bytes 589840 | tf_op jit(solution)/shard_map/psum | solution.py:119
  (403 shorter events, 304.4 us)
Async XLA Ops:
  7.2 427.4 %all-reduce.3.cloned.1.call-start = ((), (), s32[]{:S(2)}) async-start(), calls=%async_computation | async-start | bytes 1310720 | tf_op jit(solution)/shard_map/psum | solution.py:119
  8.2 10.1 %collective-permute-start.2 = (bf16[64,1,128]{2,1,0:T(2,128)(2,1)S(1)}, bf16[64,1,128]{2,1,0:T(2,128)(2,1)S(1)}, u32[]{:S(2)}, u32[]{:S(2)}) collective-permute-start(bf16[64,1,128]{2,1,0:T(2,128)(2,1)S(1)} %get-tuple-element.223), channel_id=1, source_target_pairs={{0,8},{8,16},{16,24},{24,32},{32,40},{40,48},{48,56},{1,9},{9,17},... | collective-permute-start | bytes 49160 | tf_op jit(solution)/shard_map/ppermute | solution.py:17
  21.5 10.1 %collective-permute-start.5 = (bf16[64,10,1]{2,1,0:T(8,128)(2,1)S(1)}, bf16[64,10,1]{2,1,0:T(8,128)(2,1)S(1)}, u32[]{:S(2)}, u32[]{:S(2)}) collective-permute-start(bf16[64,10,1]{2,1,0:T(8,128)(2,1)S(1)} %get-tuple-element.175), channel_id=1, source_target_pairs={{1,0},{2,1},{3,2},{4,3},{5,4},{6,5},{7,6},{9,8},{10,9},{11,10},{12... | collective-permute-start | bytes 3848 | tf_op jit(solution)/shard_map/ppermute | solution.py:19
  64.7 9.7 %collective-permute-start.12 = (bf16[64,10,1]{2,1,0:T(8,128)(2,1)S(1)}, bf16[64,10,1]{2,1,0:T(8,128)(2,1)S(1)}, u32[]{:S(2)}, u32[]{:S(2)}) collective-permute-start(bf16[64,10,1]{2,1,0:T(8,128)(2,1)S(1)} %get-tuple-element.172), channel_id=1, source_target_pairs={{0,1},{1,2},{2,3},{3,4},{4,5},{5,6},{6,7},{8,9},{9,10},{10,11},{11... | collective-permute-start | bytes 3848 | tf_op jit(solution)/shard_map/ppermute | solution.py:17
  70.8 8.9 %collective-permute-start.13 = (bf16[64,10,1]{2,1,0:T(8,128)(2,1)S(1)}, bf16[64,10,1]{2,1,0:T(8,128)(2,1)S(1)}, u32[]{:S(2)}, u32[]{:S(2)}) collective-permute-start(bf16[64,10,1]{2,1,0:T(8,128)(2,1)S(1)} %get-tuple-element.171), channel_id=1, source_target_pairs={{1,0},{2,1},{3,2},{4,3},{5,4},{6,5},{7,6},{9,8},{10,9},{11,10},{12... | collective-permute-start | bytes 3848 | tf_op jit(solution)/shard_map/ppermute | solution.py:19
  105.6 9.8 %collective-permute-start = (f32[64,1024]{1,0:T(8,128)S(1)}, f32[64,1024]{1,0:T(8,128)S(1)}, u32[]{:S(2)}, u32[]{:S(2)}) collective-permute-start(f32[64,1024]{1,0:T(8,128)S(1)} %convolution_add_fusion.4), channel_id=1, source_target_pairs={{0,64},{64,128},{128,192},{192,256},{256,320},{320,384},{384,448},... | collective-permute-start | bytes 786440 | tf_op jit(solution)/shard_map/while/body/eval_jaxpr/ppermute | solution.py:29
  115.8 9.4 %collective-permute-start = (f32[64,1024]{1,0:T(8,128)S(1)}, f32[64,1024]{1,0:T(8,128)S(1)}, u32[]{:S(2)}, u32[]{:S(2)}) collective-permute-start(f32[64,1024]{1,0:T(8,128)S(1)} %convolution_add_fusion.4), channel_id=1, source_target_pairs={{0,64},{64,128},{128,192},{192,256},{256,320},{320,384},{384,448},... | collective-permute-start | bytes 786440 | tf_op jit(solution)/shard_map/while/body/eval_jaxpr/ppermute | solution.py:29
  134.6 9.1 %collective-permute-start = (f32[64,1024]{1,0:T(8,128)S(1)}, f32[64,1024]{1,0:T(8,128)S(1)}, u32[]{:S(2)}, u32[]{:S(2)}) collective-permute-start(f32[64,1024]{1,0:T(8,128)S(1)} %convolution_add_fusion.4), channel_id=1, source_target_pairs={{0,64},{64,128},{128,192},{192,256},{256,320},{320,384},{384,448},... | collective-permute-start | bytes 786440 | tf_op jit(solution)/shard_map/while/body/eval_jaxpr/ppermute | solution.py:29
  169.5 9.0 %collective-permute-start.18 = (bf16[64,1,128]{2,1,0:T(2,128)(2,1)S(1)}, bf16[64,1,128]{2,1,0:T(2,128)(2,1)S(1)}, u32[]{:S(2)}, u32[]{:S(2)}) collective-permute-start(bf16[64,1,128]{2,1,0:T(2,128)(2,1)S(1)} %get-tuple-element.215), channel_id=1, source_target_pairs={{0,8},{8,16},{16,24},{24,32},{32,40},{40,48},{48,56},{1,9},{9,17},... | collective-permute-start | bytes 49160 | tf_op jit(solution)/shard_map/ppermute | solution.py:17
  183.3 9.5 %collective-permute-start.21 = (bf16[64,10,1]{2,1,0:T(8,128)(2,1)S(1)}, bf16[64,10,1]{2,1,0:T(8,128)(2,1)S(1)}, u32[]{:S(2)}, u32[]{:S(2)}) collective-permute-start(bf16[64,10,1]{2,1,0:T(8,128)(2,1)S(1)} %get-tuple-element.167), channel_id=1, source_target_pairs={{1,0},{2,1},{3,2},{4,3},{5,4},{6,5},{7,6},{9,8},{10,9},{11,10},{12... | collective-permute-start | bytes 3848 | tf_op jit(solution)/shard_map/ppermute | solution.py:19
  206.0 9.8 %collective-permute-start.25 = (bf16[64,10,1]{2,1,0:T(8,128)(2,1)S(1)}, bf16[64,10,1]{2,1,0:T(8,128)(2,1)S(1)}, u32[]{:S(2)}, u32[]{:S(2)}) collective-permute-start(bf16[64,10,1]{2,1,0:T(8,128)(2,1)S(1)} %get-tuple-element.165), channel_id=1, source_target_pairs={{1,0},{2,1},{3,2},{4,3},{5,4},{6,5},{7,6},{9,8},{10,9},{11,10},{12... | collective-permute-start | bytes 3848 | tf_op jit(solution)/shard_map/ppermute | solution.py:19
  231.3 8.8 %collective-permute-start.29 = (bf16[64,10,1]{2,1,0:T(8,128)(2,1)}, bf16[64,10,1]{2,1,0:T(8,128)(2,1)S(1)}, u32[]{:S(2)}, u32[]{:S(2)}) collective-permute-start(bf16[64,10,1]{2,1,0:T(8,128)(2,1)} %get-tuple-element.163), channel_id=1, source_target_pairs={{1,0},{2,1},{3,2},{4,3},{5,4},{6,5},{7,6},{9,8},{10,9},{11,10},{12... | collective-permute-start | bytes 3848 | tf_op jit(solution)/shard_map/ppermute | solution.py:19
  255.5 8.7 %collective-permute-start.33 = (bf16[64,10,1]{2,1,0:T(8,128)(2,1)}, bf16[64,10,1]{2,1,0:T(8,128)(2,1)S(1)}, u32[]{:S(2)}, u32[]{:S(2)}) collective-permute-start(bf16[64,10,1]{2,1,0:T(8,128)(2,1)} %get-tuple-element.161), channel_id=1, source_target_pairs={{1,0},{2,1},{3,2},{4,3},{5,4},{6,5},{7,6},{9,8},{10,9},{11,10},{12... | collective-permute-start | bytes 3848 | tf_op jit(solution)/shard_map/ppermute | solution.py:19
  285.0 9.3 %collective-permute-start.37 = (bf16[64,10,1]{2,1,0:T(8,128)(2,1)}, bf16[64,10,1]{2,1,0:T(8,128)(2,1)S(1)}, u32[]{:S(2)}, u32[]{:S(2)}) collective-permute-start(bf16[64,10,1]{2,1,0:T(8,128)(2,1)} %get-tuple-element.159), channel_id=1, source_target_pairs={{1,0},{2,1},{3,2},{4,3},{5,4},{6,5},{7,6},{9,8},{10,9},{11,10},{12... | collective-permute-start | bytes 3848 | tf_op jit(solution)/shard_map/ppermute | solution.py:19
  298.6 9.9 %collective-permute-start.38 = (bf16[64,1,128]{2,1,0:T(2,128)(2,1)}, bf16[64,1,128]{2,1,0:T(2,128)(2,1)S(1)}, u32[]{:S(2)}, u32[]{:S(2)}) collective-permute-start(bf16[64,1,128]{2,1,0:T(2,128)(2,1)} %get-tuple-element.205), channel_id=1, source_target_pairs={{0,8},{8,16},{16,24},{24,32},{32,40},{40,48},{48,56},{1,9},{9,17},... | collective-permute-start | bytes 49160 | tf_op jit(solution)/shard_map/ppermute | solution.py:17
  311.8 9.9 %collective-permute-start.41 = (bf16[64,10,1]{2,1,0:T(8,128)(2,1)S(1)}, bf16[64,10,1]{2,1,0:T(8,128)(2,1)S(1)}, u32[]{:S(2)}, u32[]{:S(2)}) collective-permute-start(bf16[64,10,1]{2,1,0:T(8,128)(2,1)S(1)} %get-tuple-element.157), channel_id=1, source_target_pairs={{1,0},{2,1},{3,2},{4,3},{5,4},{6,5},{7,6},{9,8},{10,9},{11,10},{12... | collective-permute-start | bytes 3848 | tf_op jit(solution)/shard_map/ppermute | solution.py:19
  334.8 9.0 %collective-permute-start.45 = (bf16[64,10,1]{2,1,0:T(8,128)(2,1)S(1)}, bf16[64,10,1]{2,1,0:T(8,128)(2,1)S(1)}, u32[]{:S(2)}, u32[]{:S(2)}) collective-permute-start(bf16[64,10,1]{2,1,0:T(8,128)(2,1)S(1)} %get-tuple-element.155), channel_id=1, source_target_pairs={{1,0},{2,1},{3,2},{4,3},{5,4},{6,5},{7,6},{9,8},{10,9},{11,10},{12... | collective-permute-start | bytes 3848 | tf_op jit(solution)/shard_map/ppermute | solution.py:19
  357.1 153.6 %all-reduce.5.cloned.1.call-start = ((), (), s32[]{:S(2)}) async-start(), calls=%async_computation.1 | async-start | bytes 1310720 | tf_op jit(solution)/shard_map/psum | solution.py:119
  357.2 9.0 %collective-permute-start.49 = (bf16[64,10,1]{2,1,0:T(8,128)(2,1)S(1)}, bf16[64,10,1]{2,1,0:T(8,128)(2,1)S(1)}, u32[]{:S(2)}, u32[]{:S(2)}) collective-permute-start(bf16[64,10,1]{2,1,0:T(8,128)(2,1)S(1)} %get-tuple-element.153), channel_id=1, source_target_pairs={{1,0},{2,1},{3,2},{4,3},{5,4},{6,5},{7,6},{9,8},{10,9},{11,10},{12... | collective-permute-start | bytes 3848 | tf_op jit(solution)/shard_map/ppermute | solution.py:19
  450.9 9.6 %collective-permute-start.1 = (f32[64,1024]{1,0:T(8,128)S(1)}, f32[64,1024]{1,0:T(8,128)S(1)}, u32[]{:S(2)}, u32[]{:S(2)}) collective-permute-start(f32[64,1024]{1,0:T(8,128)S(1)} %convolution_add_fusion.5), channel_id=1, source_target_pairs={{64,0},{128,64},{192,128},{256,192},{320,256},{384,320},{448,384},... | collective-permute-start | bytes 786440 | tf_op jit(solution)/shard_map/while/body/eval_jaxpr/ppermute | solution.py:29
  460.9 10.2 %collective-permute-start.1 = (f32[64,1024]{1,0:T(8,128)S(1)}, f32[64,1024]{1,0:T(8,128)S(1)}, u32[]{:S(2)}, u32[]{:S(2)}) collective-permute-start(f32[64,1024]{1,0:T(8,128)S(1)} %convolution_add_fusion.5), channel_id=1, source_target_pairs={{64,0},{128,64},{192,128},{256,192},{320,256},{384,320},{448,384},... | collective-permute-start | bytes 786440 | tf_op jit(solution)/shard_map/while/body/eval_jaxpr/ppermute | solution.py:29
  471.4 9.3 %collective-permute-start.1 = (f32[64,1024]{1,0:T(8,128)S(1)}, f32[64,1024]{1,0:T(8,128)S(1)}, u32[]{:S(2)}, u32[]{:S(2)}) collective-permute-start(f32[64,1024]{1,0:T(8,128)S(1)} %convolution_add_fusion.5), channel_id=1, source_target_pairs={{64,0},{128,64},{192,128},{256,192},{320,256},{384,320},{448,384},... | collective-permute-start | bytes 786440 | tf_op jit(solution)/shard_map/while/body/eval_jaxpr/ppermute | solution.py:29
  481.1 9.3 %collective-permute-start.1 = (f32[64,1024]{1,0:T(8,128)S(1)}, f32[64,1024]{1,0:T(8,128)S(1)}, u32[]{:S(2)}, u32[]{:S(2)}) collective-permute-start(f32[64,1024]{1,0:T(8,128)S(1)} %convolution_add_fusion.5), channel_id=1, source_target_pairs={{64,0},{128,64},{192,128},{256,192},{320,256},{384,320},{448,384},... | collective-permute-start | bytes 786440 | tf_op jit(solution)/shard_map/while/body/eval_jaxpr/ppermute | solution.py:29
  490.7 11.4 %collective-permute-start.1 = (f32[64,1024]{1,0:T(8,128)S(1)}, f32[64,1024]{1,0:T(8,128)S(1)}, u32[]{:S(2)}, u32[]{:S(2)}) collective-permute-start(f32[64,1024]{1,0:T(8,128)S(1)} %convolution_add_fusion.5), channel_id=1, source_target_pairs={{64,0},{128,64},{192,128},{256,192},{320,256},{384,320},{448,384},... | collective-permute-start | bytes 786440 | tf_op jit(solution)/shard_map/while/body/eval_jaxpr/ppermute | solution.py:29
  (67 other events, 430.7 us)
Sparse Core Ops, SparseCore 0:
  357.3 77.2 all-reduce.2
  436.9 73.7 all-reduce.4
